TPU v7x, 32 devices: a whole 2x2x4 slice. The times are simulated.
32 devices in a mesh: aux: 4 (over y, x), row: 8 (over z, core).
Axes of the slice: x: 2, y: 2, z: 4, core: 2. Of those that a mesh axis runs over, the one named last changes fastest.
Arguments:
- coeff: bfloat16 [800, 1024], P(None, 'row'), may hold values from -0.109375 to 0.109375
- band: bfloat16 [8, 384, 1024], P('aux', None, 'row'), may hold values from -6 to 6
- pairs: int32 [8, 8], replicated, may hold values from 0 to 1, as said below
Outputs:
- exchange_k: float32 [1024, 1024], P('row', 'aux')
Inputs may be any that keep to these rules, and one draw needn't show every extreme that they name: pairs is symmetric, holds only 0 and 1, and its diagonal is 1; how many blocks a row keeps differs from row to row.
All inputs are finite; a program needn't handle non-finite values.
Results may differ from a plain program's by a relative error of at most 0.0012.
Values may be sent and summed in bfloat16 or wider, within the bound.
A program may use at most 64 MiB of HBM per device.

v0:
```python
import jax
import jax.numpy as jnp
from jax import lax
from jax.sharding import PartitionSpec as P


def padded_2(cells, sides, width):
    for axis, dim in sides:
        count = lax.axis_size(axis)
        ends = count - 1
        head = lax.slice_in_dim(cells, 0, width, axis=dim)
        tail = lax.slice_in_dim(cells, cells.shape[dim] - width, cells.shape[dim], axis=dim)
        cells = jnp.concatenate(
            [
                lax.ppermute(tail, axis, [(i, (i + 1) % count) for i in range(ends)]),
                cells,
                lax.ppermute(head, axis, [((i + 1) % count, i) for i in range(ends)]),
            ],
            axis=dim,
        )
    return cells


def on_device(coeff, band, pairs):
    block = band.shape[2]
    row_count = lax.axis_size("row")
    own_index = lax.axis_index("row")
    padded = padded_2(coeff, (("row", 1),), block)
    half_factor = jnp.einsum(
        "ij,qjm->qim", padded, band, preferred_element_type=jnp.float32
    ).astype(jnp.bfloat16)
    stacked = half_factor.reshape(-1, block)
    own_row = lax.dynamic_index_in_dim(pairs, own_index, 0, keepdims=False)
    piece = lax.all_gather(stacked, "row", axis=1, tiled=True)
    product = lax.dot_general(
        stacked, piece, (((0,), (0,)), ((), ())), preferred_element_type=jnp.float32
    )
    column_block = jnp.arange(piece.shape[1], dtype=jnp.int32) // block
    onehot = (column_block[:, None] == jnp.arange(row_count, dtype=jnp.int32)[None, :]).astype(
        jnp.float32
    )
    screen = jnp.dot(onehot, own_row.astype(jnp.float32))
    k_rows = product * screen[None, :]
    return lax.psum_scatter(k_rows, "aux", scatter_dimension=1, tiled=True)


def solution(mesh):
    placed = (P(None, "row"), P("aux", None, "row"), P())
    return jax.shard_map(
        on_device, mesh=mesh, in_specs=placed, out_specs=P("row", "aux"), check_vma=False
    )
```

profile of v0, /device:TPU:0, one launch (start us, length us, event | category | flops | bytes accessed | tf_op | source)
XLA Modules:
  0.0 95.0 jit_solution(17839355285652718635)
XLA Ops:
  6.5 0.0 copy-start
  6.5 0.0 all-gather.2.cloned.1.call-start
  6.5 2.5 %collective-permute-start = (bf16[800,128]{1,0:T(8,128)(2,1)}, bf16[800,128]{1,0:T(8,128)(2,1)S(1)}, u32[]{:S(2)}, u32[]{:S(2)}) collective-permute-start(bf16[800,128]{1,0:T(8,128)(2,1)} %param.3), channel_id=1, source_target_pairs={{0,1},{1,2},{2,3},{3,4},{4,5},{5,6},{6,7},{8,9},{9,10},{10,11},{11... | collective-permute-start | bytes 614408 | tf_op jit(solution)/shard_map/ppermute | solution.py:15
  9.0 1.3 %collective-permute-start.1 = (bf16[800,128]{1,0:T(8,128)(2,1)}, bf16[800,128]{1,0:T(8,128)(2,1)S(1)}, u32[]{:S(2)}, u32[]{:S(2)}) collective-permute-start(bf16[800,128]{1,0:T(8,128)(2,1)} %param.3), channel_id=1, source_target_pairs={{1,0},{2,1},{3,2},{4,3},{5,4},{6,5},{7,6},{9,8},{10,9},{11,10},{12... | collective-permute-start | bytes 614408 | tf_op jit(solution)/shard_map/ppermute | solution.py:17
  10.3 0.0 collective-permute-done
  10.3 4.4 %collective-permute-done.1 = bf16[800,128]{1,0:T(8,128)(2,1)S(1)} collective-permute-done((bf16[800,128]{1,0:T(8,128)(2,1)}, bf16[800,128]{1,0:T(8,128)(2,1)S(1)}, u32[]{:S(2)}, u32[]{:S(2)}) %collective-permute-start.1) | collective-permute-done | bytes 204832 | tf_op jit(solution)/shard_map/ppermute | solution.py:17
  14.8 0.0 copy-done
  14.8 2.1 %convolution_convert_fusion = bf16[800,2,128]{2,0,1:T(8,128)(2,1)} fusion(bf16[2,384,128]{2,1,0:T(8,128)(2,1)S(1)} %copy-done, bf16[800,128]{1,0:T(8,128)(2,1)S(1)} %collective-permute-done.1, bf16[800,128]{1,0:T(8,128)(2,1)} %param.3, bf16[800,128]{1,0:T(8,128)(2,1)S(1)} %collective-permute-done), kind=kOutput, calls=%fused_computation | convolution fusion | flops 159334400 | bytes 1220608 | tf_op jit(solution)/shard_map/ij,qjm->qim/dot_general | solution.py:29
  16.8 0.0 all-gather.2.cloned.1.call-update
  16.9 0.0 reduce-scatter.2.cloned.1.call-start
  16.9 1.0 %fusion.4 = f32[1,1024]{1,0:T(1,128)S(1)} fusion(s32[1024]{0:T(1024)S(1)} %add_select_fusion, s32[8,8]{1,0:T(8,128)} %param.5, s32[]{:T(128)S(6)} %select_n.14), kind=kOutput, calls=%fused_computation.8 | convolution fusion | flops 24584 | bytes 8708 | tf_op jit(solution)/shard_map/dot_general | solution.py:42
  17.9 43.5 %all-gather.2.cloned.1.call-done = bf16[1600,1024]{1,0:T(8,128)(2,1)} async-done(((bf16[1600,128]{1,0:T(8,128)(2,1)}), bf16[1600,1024]{1,0:T(8,128)(2,1)}) %all-gather.2.cloned.1.call-update) | async-done | bytes 3276816 | tf_op jit(solution)/shard_map/all_gather | solution.py:34
  61.4 3.5 %convolution_multiply_fusion = f32[128,1024]{1,0:T(8,128)} fusion(bf16[1600,128]{1,0:T(8,128)(2,1)} %bitcast.15, bf16[1600,1024]{1,0:T(8,128)(2,1)} %all-gather.2.cloned.1.call-done, f32[1024]{0:T(1024)S(1)} %bitcast.16), kind=kOutput, calls=%fused_computation.1 | convolution fusion | flops 419561472 | bytes 4214784 | tf_op jit(solution)/shard_map/dot_general | solution.py:35
  64.9 0.0 reduce-scatter.2.cloned.1.call-update
  65.0 23.2 %reduce-scatter.2.cloned.1.call-done = f32[128,256]{1,0:T(8,128)} async-done(((f32[128,1024]{1,0:T(8,128)}), f32[128,256]{1,0:T(8,128)}) %reduce-scatter.2.cloned.1.call-update) | async-done | bytes 131088 | tf_op jit(solution)/shard_map/reduce_scatter | solution.py:44
  (1 shorter events, 0.0 us)
Async XLA Ops:
  6.5 8.2 %copy-start = (bf16[2,384,128]{2,1,0:T(8,128)(2,1)S(1)}, bf16[2,384,128]{2,1,0:T(8,128)(2,1)}, u32[]{:S(2)}) copy-start(bf16[2,384,128]{2,1,0:T(8,128)(2,1)} %param.4) | copy-start | bytes 589828
  6.5 54.8 %all-gather.2.cloned.1.call-start = ((), (), s32[]{:S(2)}) async-start(), calls=%async_computation.1 | async-start | bytes 3686400 | tf_op jit(solution)/shard_map/all_gather | solution.py:34
  6.5 3.8 %collective-permute-start = (bf16[800,128]{1,0:T(8,128)(2,1)}, bf16[800,128]{1,0:T(8,128)(2,1)S(1)}, u32[]{:S(2)}, u32[]{:S(2)}) collective-permute-start(bf16[800,128]{1,0:T(8,128)(2,1)} %param.3), channel_id=1, source_target_pairs={{0,1},{1,2},{2,3},{3,4},{4,5},{5,6},{6,7},{8,9},{9,10},{10,11},{11... | collective-permute-start | bytes 614408 | tf_op jit(solution)/shard_map/ppermute | solution.py:15
  9.0 5.7 %collective-permute-start.1 = (bf16[800,128]{1,0:T(8,128)(2,1)}, bf16[800,128]{1,0:T(8,128)(2,1)S(1)}, u32[]{:S(2)}, u32[]{:S(2)}) collective-permute-start(bf16[800,128]{1,0:T(8,128)(2,1)} %param.3), channel_id=1, source_target_pairs={{1,0},{2,1},{3,2},{4,3},{5,4},{6,5},{7,6},{9,8},{10,9},{11,10},{12... | collective-permute-start | bytes 614408 | tf_op jit(solution)/shard_map/ppermute | solution.py:17
  16.9 71.3 %reduce-scatter.2.cloned.1.call-start = ((), (), s32[]{:S(2)}) async-start(), calls=%async_computation.2 | async-start | bytes 655360 | tf_op jit(solution)/shard_map/reduce_scatter | solution.py:44
Sparse Core Ops, SparseCore 0:
  17.0 44.3 all-gather.1
  65.1 23.0 reduce-scatter.1
where the time goes:
time: 95.2 us; the launch traced here: 95 us
  waiting for transfers between devices  71.1 us (75%)
  between operations  13.4 us (14%)
  matrix products  6.61 us (7%)
  starting transfers between devices  3.82 us (4%)
    all_gather x1, waiting for transfers between devices, on_device(): piece = lax.all_gather(stacked, 'row', axis=1, tiled=True)  43.5 us
    reduce_scatter x1, waiting for transfers between devices, on_device(): return lax.psum_scatter(k_rows, 'aux', scatter_dimension=1, tiled=True)  23.2 us
    ppermute x1, waiting for transfers between devices, padded_2(): lax.ppermute(head, axis, [((i + 1) % count, i) for i in range(ends)])  4.43 us
    dot_general x1, matrix products, on_device(): lax.dot_general(stacked, piece, (((0,), (0,)), ((), ())), preferred_eleme...  3.55 us
    ppermute x1, starting transfers between devices, padded_2(): lax.ppermute(tail, axis, [(i, (i + 1) % count) for i in range(ends)])  2.49 us
    dot_general x1, matrix products, on_device(): jnp.einsum('ij,qjm->qim', padded, band, preferred_element_type=jnp.float32)  2.06 us
  transfers between devices with their start and end apart: 4, of which 3 were waited for; matrix products, arithmetic and copies ran while one was open for 1% of the time, Pallas kernels for 0%

commit v1 on v0

v1 whole, which is shorter than its diff:
```python
import functools

import jax
import jax.numpy as jnp
from jax import lax
from jax.experimental import pallas as pl
from jax.experimental.pallas import tpu as pltpu
from jax.sharding import PartitionSpec as P

MESH = pl.DeviceIdType.MESH


def exchange_kernel(
    rows, groups, coeff_ref, band_ref, pairs_ref, out_ref,
    coeffs, bands, halves, own_t, parts, arrived,
    cz_send, cs_send, ca_send, c_recv, bz_send, bs_send, b_recv, k_send, k_recv,
):
    chips = rows // 2
    occupied, block = coeff_ref.shape
    naux = band_ref.shape[0]
    piece = occupied // 2
    group = lax.axis_index("aux")
    row = lax.axis_index("row")
    chip, core = row // 2, row % 2
    other = chip * 2 + (1 - core)

    def each_side(act):
        for side, step in ((0, 1), (1, -1)):
            target = chip + step
            pl.when((target >= 0) & (target < chips))(
                functools.partial(act, side, target * 2 + core)
            )

    barrier = pltpu.get_barrier_semaphore()

    def greet(side, target):
        pl.semaphore_signal(barrier, inc=1, device_id={"row": target}, device_id_type=MESH)

    each_side(greet)
    pl.semaphore_signal(barrier, inc=1, device_id={"row": other}, device_id_type=MESH)
    for shift in range(1, groups):
        pl.semaphore_signal(
            barrier, inc=1, device_id={"aux": lax.rem(group + shift, groups)}, device_id_type=MESH
        )

    edge = jnp.zeros((occupied, block), coeffs.dtype)
    coeffs[:, :block] = edge
    coeffs[:, (rows + 1) * block:] = edge
    coeffs[:, pl.ds(pl.multiple_of((row + 1) * block, block), block)] = coeff_ref[...]
    bands[row] = band_ref[...]

    sides = jnp.minimum(chip, 1) + jnp.minimum(chips - 1 - chip, 1)
    pl.semaphore_wait(barrier, groups + sides)

    def slot(owner, part):
        return coeffs.at[
            pl.ds(part * piece, piece),
            pl.ds(pl.multiple_of((owner + 1) * block, block), block),
        ]

    def send(src, dst, sent, got, where):
        return pltpu.make_async_remote_copy(
            src_ref=src, dst_ref=dst, send_sem=sent, recv_sem=got,
            device_id=where, device_id_type=MESH,
        )

    def coeff_on(owner, part, side, target):
        return send(slot(owner, part), slot(owner, part), cz_send.at[side, owner, part],
                    c_recv.at[owner, part], {"row": target})

    def coeff_other(owner, part):
        return send(slot(owner, part), slot(owner, part), cs_send.at[owner, part],
                    c_recv.at[owner, part], {"row": other})

    def coeff_aux(owner, part, shift):
        return send(slot(owner, part), slot(owner, part), ca_send.at[owner // 2, part, shift - 1],
                    c_recv.at[owner, part], {"aux": lax.rem(group + shift, groups)})

    def band_on(owner, q, side, target):
        return send(bands.at[owner, q], bands.at[owner, q], bz_send.at[side, owner, q],
                    b_recv.at[owner, q], {"row": target})

    def band_other(owner, q):
        return send(bands.at[owner, q], bands.at[owner, q], bs_send.at[owner, q],
                    b_recv.at[owner, q], {"row": other})

    def carries(owner, part):
        return lax.rem(owner * 2 + part, groups) == group

    def part_out(to):
        return send(parts.at[to], arrived.at[group], k_send.at[to], k_recv.at[group], {"aux": to})

    def start_coeff(side, target):
        for part in range(2):
            pl.when(carries(row, part))(
                lambda part=part: coeff_on(row, part, side, target).start()
            )

    def start_band(side, target):
        for q in range(naux):
            band_on(row, q, side, target).start()

    each_side(start_coeff)
    for part in range(2):
        coeff_other(row, part).start()
    each_side(start_band)
    for q in range(naux):
        band_other(row, q).start()

    def sources(step):
        return ((0, chip - step, chip + 1), (1, chip + step, chip - 1))

    def inside(index):
        return (index >= 0) & (index < chips)

    def relay_coeff(step):
        for side, origin, ahead in sources(step):
            @pl.when(inside(origin))
            def _():
                owner = origin * 2 + core
                for part in range(2):
                    coeff_other(owner, part).wait_recv()

                    @pl.when(carries(owner, part))
                    def _():
                        pl.when(inside(ahead))(
                            lambda: coeff_on(owner, part, side, ahead * 2 + core).start()
                        )
                        for shift in range(1, groups):
                            coeff_aux(owner, part, shift).start()

                    coeff_other(owner, part).start()

    def relay_band(step):
        for side, origin, ahead in sources(step):
            @pl.when(inside(origin))
            def _():
                owner = origin * 2 + core
                for q in range(naux):
                    band_other(owner, q).wait_recv()
                    pl.when(inside(ahead))(
                        lambda: band_on(owner, q, side, ahead * 2 + core).start()
                    )
                    band_other(owner, q).start()

    def other_coeff(step):
        for side, origin, ahead in sources(step):
            @pl.when(inside(origin))
            def _():
                for part in range(2):
                    coeff_other(origin * 2 + 1 - core, part).wait_recv()

    def half_pair(origin):
        for j in range(2):
            owner = origin * 2 + j
            window = coeffs[:, pl.ds(pl.multiple_of(owner * block, block), 3 * block)]
            slab = jnp.concatenate([bands[owner, q] for q in range(naux)], axis=1)
            halves[j] = jnp.dot(window, slab, preferred_element_type=jnp.float32).astype(
                halves.dtype
            )

    def multiply(origin):
        total = None
        for q in range(naux):
            cut = slice(q * block, (q + 1) * block)
            both = jnp.concatenate([halves[0, :, cut], halves[1, :, cut]], axis=1)
            term = jnp.dot(own_t[cut, :], both, preferred_element_type=jnp.float32)
            total = term if total is None else total + term
        parts[origin] = total
        pl.when(origin != group)(lambda: part_out(origin).start())

    relay_coeff(1)
    relay_band(1)
    for part in range(2):
        coeff_other(other, part).wait_recv()
    other_coeff(1)
    for q in range(naux):
        band_other(other, q).wait_recv()
    half_pair(chip)
    own_t[...] = halves[core].T
    multiply(chip)

    def forward(step, carry):
        @pl.when(step + 1 < chips)
        def _():
            relay_coeff(step + 1)
            other_coeff(step + 1)

        for side, origin, ahead in sources(step):
            @pl.when(inside(origin))
            def _():
                for q in range(naux):
                    band_other(origin * 2 + 1 - core, q).wait_recv()
                half_pair(origin)
                multiply(origin)

        pl.when(step + 1 < chips)(lambda: relay_band(step + 1))
        return carry

    lax.fori_loop(1, chips, forward, 0)

    total = parts[group]
    for shift in range(1, groups):
        giver = lax.rem(group + shift, groups)
        send(parts.at[giver], arrived.at[giver], k_send.at[giver], k_recv.at[giver],
             {"aux": giver}).wait_recv()
        total = total + arrived[giver]
    for j in range(2):
        kept = pairs_ref[row, group * 2 + j].astype(jnp.float32)
        out_ref[:, j * block:(j + 1) * block] = total[:, j * block:(j + 1) * block] * kept

    def left_own(side, target):
        for part in range(2):
            pl.when(carries(row, part))(
                lambda part=part: coeff_on(row, part, side, target).wait_send()
            )
        for q in range(naux):
            band_on(row, q, side, target).wait_send()

    each_side(left_own)
    for part in range(2):
        coeff_other(row, part).wait_send()
    for q in range(naux):
        band_other(row, q).wait_send()

    def left(step, carry):
        for side, origin, ahead in sources(step):
            @pl.when(inside(origin))
            def _():
                owner = origin * 2 + core
                for part in range(2):
                    @pl.when(carries(owner, part))
                    def _():
                        pl.when(inside(ahead))(
                            lambda: coeff_on(owner, part, side, ahead * 2 + core).wait_send()
                        )
                        for shift in range(1, groups):
                            coeff_aux(owner, part, shift).wait_send()

                    coeff_other(owner, part).wait_send()
                for q in range(naux):
                    pl.when(inside(ahead))(
                        lambda: band_on(owner, q, side, ahead * 2 + core).wait_send()
                    )
                    band_other(owner, q).wait_send()

        return carry

    lax.fori_loop(1, chips, left, 0)
    for shift in range(1, groups):
        part_out(lax.rem(group + shift, groups)).wait_send()


def on_device(rows, groups, coeff, band, pairs):
    occupied, block = coeff.shape
    naux, depth, _ = band.shape
    chips = rows // 2
    dma = pltpu.SemaphoreType.DMA
    vmem = pl.BlockSpec(memory_space=pltpu.VMEM)
    flops = 2 * rows * naux * occupied * block * (depth + block)
    return pl.pallas_call(
        functools.partial(exchange_kernel, rows, groups),
        out_shape=jax.ShapeDtypeStruct((block, 2 * block), jnp.float32),
        in_specs=[vmem, vmem, pl.BlockSpec(memory_space=pltpu.SMEM)],
        out_specs=vmem,
        scratch_shapes=[
            pltpu.VMEM((occupied, (rows + 2) * block), jnp.bfloat16),
            pltpu.VMEM((rows, naux, depth, block), jnp.bfloat16),
            pltpu.VMEM((2, occupied, naux * block), jnp.bfloat16),
            pltpu.VMEM((naux * block, occupied), jnp.bfloat16),
            pltpu.VMEM((groups, block, 2 * block), jnp.float32),
            pltpu.VMEM((groups, block, 2 * block), jnp.float32),
            dma((2, rows, 2)), dma((rows, 2)), dma((chips, 2, groups - 1)), dma((rows, 2)),
            dma((2, rows, naux)), dma((rows, naux)), dma((rows, naux)),
            dma((groups,)), dma((groups,)),
        ],
        compiler_params=pltpu.CompilerParams(
            collective_id=0, has_side_effects=True, vmem_limit_bytes=48 * 2**20
        ),
        cost_estimate=pl.CostEstimate(flops=flops, bytes_accessed=2**20, transcendentals=0),
    )(coeff, band, pairs)


def solution(mesh):
    rows, groups = mesh.shape["row"], mesh.shape["aux"]
    placed = (P(None, "row"), P("aux", None, "row"), P())
    return jax.shard_map(
        functools.partial(on_device, rows, groups),
        mesh=mesh, in_specs=placed, out_specs=P("row", "aux"), check_vma=False,
    )
```

time: 95.2 us -> 57.2 us (0.60)
  waiting for transfers between devices: 71.1 us -> 0 us
  Pallas kernels: 0 us -> 53.8 us
  between operations: 13.4 us -> 0.01 us
  matrix products: 6.61 us -> 0 us
  starting transfers between devices: 3.82 us -> 0 us
  local copies, waits for them, and re-layouts: 0.01 us -> 3.2 us
    pallas_call x0 -> x1, Pallas kernels: none -> 53.8 us  [on_device(): pl.pallas_call(functools.partial(exchange_kernel, rows, groups), out_shap...]
    all_gather x1 -> x0, waiting for transfers between devices: 43.5 us -> none  [on_device(): piece = lax.all_gather(stacked, 'row', axis=1, tiled=True)]
    reduce_scatter x1 -> x0, waiting for transfers between devices: 23.2 us -> none  [on_device(): return lax.psum_scatter(k_rows, 'aux', scatter_dimension=1, tiled=True)]
    dot_general x3 -> x0, matrix products: 6.61 us -> none  [the longest x1 3.55 us: on_device(): lax.dot_general(stacked, piece, (((0,), (0,)), ((), ())), preferred_eleme...]
    ppermute x2 -> x0, waiting for transfers between devices: 4.43 us -> none  [the longest x1 4.43 us: padded_2(): lax.ppermute(head, axis, [((i + 1) % count, i) for i in range(ends)])]
    ppermute x2 -> x0, starting transfers between devices: 3.78 us -> none  [the longest x1 2.49 us: padded_2(): lax.ppermute(tail, axis, [(i, (i + 1) % count) for i in range(ends)])]
    unnamed x2 -> x7, local copies, waits for them, and re-layouts: 0.01 us -> 3.2 us
  transfers between devices with their start and end apart: 4 -> 0, of which waited for: 3 -> 0; matrix products, arithmetic and copies ran while one was open for 1% -> 0% of each run, Pallas kernels for 0% -> 0%
where the time goes in v1:
time: 57.2 us; the launch traced here: 57 us
  Pallas kernels  53.8 us (94%)
  local copies, waits for them, and re-layouts  3.2 us (6%)
    pallas_call x1, Pallas kernels, on_device(): pl.pallas_call(functools.partial(exchange_kernel, rows, groups), out_shap...  53.8 us
    unnamed x7, local copies, waits for them, and re-layouts  3.2 us

profile of v1, /device:TPU:0, one launch (start us, length us, event | category | flops | bytes accessed | tf_op | source)
XLA Modules:
  0.0 57.0 jit_solution(18187492299574919303)
XLA Ops:
  0.0 0.0 copy-start
  0.0 0.9 %copy-done = bf16[800,128]{1,0:T(8,128)(2,1)S(1)} copy-done((bf16[800,128]{1,0:T(8,128)(2,1)S(1)}, bf16[800,128]{1,0:T(8,128)(2,1)}, u32[]{:S(2)}) %copy-start) | copy-done | bytes 204824
  0.9 0.0 copy-start.1
  0.9 0.9 %copy-done.1 = bf16[2,384,128]{2,1,0:T(8,128)(2,1)S(1)} copy-done((bf16[2,384,128]{2,1,0:T(8,128)(2,1)S(1)}, bf16[2,384,128]{2,1,0:T(8,128)(2,1)}, u32[]{:S(2)}) %copy-start.1) | copy-done | bytes 196632
  1.9 0.0 copy-start.2
  1.9 0.7 %copy-done.2 = s32[8,8]{1,0:T(8,128)S(1)} copy-done((s32[8,8]{1,0:T(8,128)S(1)}, s32[8,8]{1,0:T(8,128)}, u32[]{:S(2)}) %copy-start.2) | copy-done | bytes 280
  2.5 53.8 %shard_map.37 = f32[128,256]{1,0:T(8,128)S(1)} custom-call(bf16[800,128]{1,0:T(8,128)(2,1)S(1)} %copy-done, bf16[2,384,128]{2,1,0:T(8,128)(2,1)S(1)} %copy-done.1, s32[8,8]{1,0:T(8,128)S(1)} %copy-done.2), custom_call_target="tpu_custom_call" | custom-call | flops 1677721600 | bytes 1048576 | tf_op jit(solution)/shard_map/pallas_call | solution.py:261
  56.4 0.7 %copy.5 = f32[128,256]{1,0:T(8,128)} copy(f32[128,256]{1,0:T(8,128)S(1)} %shard_map.37) | data formatting | bytes 262144
Async XLA Ops:
  0.0 0.9 %copy-start = (bf16[800,128]{1,0:T(8,128)(2,1)S(1)}, bf16[800,128]{1,0:T(8,128)(2,1)}, u32[]{:S(2)}) copy-start(bf16[800,128]{1,0:T(8,128)(2,1)} %coeff_ref.1) | copy-start | bytes 614404
  0.9 0.9 %copy-start.1 = (bf16[2,384,128]{2,1,0:T(8,128)(2,1)S(1)}, bf16[2,384,128]{2,1,0:T(8,128)(2,1)}, u32[]{:S(2)}) copy-start(bf16[2,384,128]{2,1,0:T(8,128)(2,1)} %band_ref.1) | copy-start | bytes 589828
  1.9 0.7 %copy-start.2 = (s32[8,8]{1,0:T(8,128)S(1)}, s32[8,8]{1,0:T(8,128)}, u32[]{:S(2)}) copy-start(s32[8,8]{1,0:T(8,128)} %pairs_ref.1) | copy-start | bytes 772

commit v2 on v1

--- a/solution.py
+++ b/solution.py
@@ -44,19 +44,16 @@
         )
 
     edge = jnp.zeros((occupied, block), coeffs.dtype)
-    coeffs[:, :block] = edge
-    coeffs[:, (rows + 1) * block:] = edge
-    coeffs[:, pl.ds(pl.multiple_of((row + 1) * block, block), block)] = coeff_ref[...]
+    coeffs[0] = edge
+    coeffs[rows + 1] = edge
+    coeffs[row + 1] = coeff_ref[...]
     bands[row] = band_ref[...]
 
     sides = jnp.minimum(chip, 1) + jnp.minimum(chips - 1 - chip, 1)
     pl.semaphore_wait(barrier, groups + sides)
 
     def slot(owner, part):
-        return coeffs.at[
-            pl.ds(part * piece, piece),
-            pl.ds(pl.multiple_of((owner + 1) * block, block), block),
-        ]
+        return coeffs.at[owner + 1, pl.ds(part * piece, piece)]
 
     def send(src, dst, sent, got, where):
         return pltpu.make_async_remote_copy(
@@ -113,25 +110,22 @@
     def inside(index):
         return (index >= 0) & (index < chips)
 
-    def relay_coeff(step):
-        for side, origin, ahead in sources(step):
-            @pl.when(inside(origin))
-            def _():
-                owner = origin * 2 + core
-                for part in range(2):
-                    coeff_other(owner, part).wait_recv()
-
+    def relay_row(step):
+        for side, origin, ahead in sources(step):
+            @pl.when(inside(origin))
+            def _():
+                owner = origin * 2 + core
+                for part in range(2):
                     @pl.when(carries(owner, part))
                     def _():
+                        coeff_other(owner, part).wait_recv()
                         pl.when(inside(ahead))(
                             lambda: coeff_on(owner, part, side, ahead * 2 + core).start()
                         )
                         for shift in range(1, groups):
                             coeff_aux(owner, part, shift).start()
-
-                    coeff_other(owner, part).start()
-
-    def relay_band(step):
+                        coeff_other(owner, part).start()
+
         for side, origin, ahead in sources(step):
             @pl.when(inside(origin))
             def _():
@@ -143,7 +137,17 @@
                     )
                     band_other(owner, q).start()
 
-    def other_coeff(step):
+    def relay_groups(step):
+        for side, origin, ahead in sources(step):
+            @pl.when(inside(origin))
+            def _():
+                owner = origin * 2 + core
+                for part in range(2):
+                    @pl.when(jnp.logical_not(carries(owner, part)))
+                    def _():
+                        coeff_other(owner, part).wait_recv()
+                        coeff_other(owner, part).start()
+
         for side, origin, ahead in sources(step):
             @pl.when(inside(origin))
             def _():
@@ -153,7 +157,7 @@
     def half_pair(origin):
         for j in range(2):
             owner = origin * 2 + j
-            window = coeffs[:, pl.ds(pl.multiple_of(owner * block, block), 3 * block)]
+            window = jnp.concatenate([coeffs[owner + near] for near in range(3)], axis=1)
             slab = jnp.concatenate([bands[owner, q] for q in range(naux)], axis=1)
             halves[j] = jnp.dot(window, slab, preferred_element_type=jnp.float32).astype(
                 halves.dtype
@@ -169,11 +173,11 @@
         parts[origin] = total
         pl.when(origin != group)(lambda: part_out(origin).start())
 
-    relay_coeff(1)
-    relay_band(1)
+    for step in range(1, min(chips, 3)):
+        relay_row(step)
     for part in range(2):
         coeff_other(other, part).wait_recv()
-    other_coeff(1)
+    relay_groups(1)
     for q in range(naux):
         band_other(other, q).wait_recv()
     half_pair(chip)
@@ -181,10 +185,8 @@
     multiply(chip)
 
     def forward(step, carry):
-        @pl.when(step + 1 < chips)
-        def _():
-            relay_coeff(step + 1)
-            other_coeff(step + 1)
+        pl.when(step + 2 < chips)(lambda: relay_row(step + 2))
+        pl.when(step + 1 < chips)(lambda: relay_groups(step + 1))
 
         for side, origin, ahead in sources(step):
             @pl.when(inside(origin))
@@ -194,7 +196,6 @@
                 half_pair(origin)
                 multiply(origin)
 
-        pl.when(step + 1 < chips)(lambda: relay_band(step + 1))
         return carry
 
     lax.fori_loop(1, chips, forward, 0)
@@ -264,7 +265,7 @@
         in_specs=[vmem, vmem, pl.BlockSpec(memory_space=pltpu.SMEM)],
         out_specs=vmem,
         scratch_shapes=[
-            pltpu.VMEM((occupied, (rows + 2) * block), jnp.bfloat16),
+            pltpu.VMEM((rows + 2, occupied, block), jnp.bfloat16),
             pltpu.VMEM((rows, naux, depth, block), jnp.bfloat16),
             pltpu.VMEM((2, occupied, naux * block), jnp.bfloat16),
             pltpu.VMEM((naux * block, occupied), jnp.bfloat16),

time: 57.2 us -> 40.9 us (0.72)
  the two profiles are of different devices: /device:TPU:0 before, /device:TPU:25 now
where the time goes in v2:
time: 40.9 us; the launch traced here: 40.7 us
  Pallas kernels  37.5 us (92%)
  local copies, waits for them, and re-layouts  3.2 us (8%)
    pallas_call x1, Pallas kernels, on_device(): pl.pallas_call(functools.partial(exchange_kernel, rows, groups), out_shap...  37.5 us
    unnamed x7, local copies, waits for them, and re-layouts  3.2 us

profile of v2, /device:TPU:25, one launch (start us, length us, event | category | flops | bytes accessed | tf_op | source)
XLA Modules:
  0.0 40.7 jit_solution(17419218801664476592)
XLA Ops:
  0.0 0.0 copy-start
  0.0 0.9 %copy-done = bf16[800,128]{1,0:T(8,128)(2,1)S(1)} copy-done((bf16[800,128]{1,0:T(8,128)(2,1)S(1)}, bf16[800,128]{1,0:T(8,128)(2,1)}, u32[]{:S(2)}) %copy-start) | copy-done | bytes 204824
  0.9 0.0 copy-start.1
  0.9 0.9 %copy-done.1 = bf16[2,384,128]{2,1,0:T(8,128)(2,1)S(1)} copy-done((bf16[2,384,128]{2,1,0:T(8,128)(2,1)S(1)}, bf16[2,384,128]{2,1,0:T(8,128)(2,1)}, u32[]{:S(2)}) %copy-start.1) | copy-done | bytes 196632
  1.9 0.0 copy-start.2
  1.9 0.7 %copy-done.2 = s32[8,8]{1,0:T(8,128)S(1)} copy-done((s32[8,8]{1,0:T(8,128)S(1)}, s32[8,8]{1,0:T(8,128)}, u32[]{:S(2)}) %copy-start.2) | copy-done | bytes 280
  2.5 37.5 %shard_map.37 = f32[128,256]{1,0:T(8,128)S(1)} custom-call(bf16[800,128]{1,0:T(8,128)(2,1)S(1)} %copy-done, bf16[2,384,128]{2,1,0:T(8,128)(2,1)S(1)} %copy-done.1, s32[8,8]{1,0:T(8,128)S(1)} %copy-done.2), custom_call_target="tpu_custom_call" | custom-call | flops 1677721600 | bytes 1048576 | tf_op jit(solution)/shard_map/pallas_call | solution.py:262
  40.0 0.7 %copy.5 = f32[128,256]{1,0:T(8,128)} copy(f32[128,256]{1,0:T(8,128)S(1)} %shard_map.37) | data formatting | bytes 262144
Async XLA Ops:
  0.0 0.9 %copy-start = (bf16[800,128]{1,0:T(8,128)(2,1)S(1)}, bf16[800,128]{1,0:T(8,128)(2,1)}, u32[]{:S(2)}) copy-start(bf16[800,128]{1,0:T(8,128)(2,1)} %coeff_ref.1) | copy-start | bytes 614404
  0.9 0.9 %copy-start.1 = (bf16[2,384,128]{2,1,0:T(8,128)(2,1)S(1)}, bf16[2,384,128]{2,1,0:T(8,128)(2,1)}, u32[]{:S(2)}) copy-start(bf16[2,384,128]{2,1,0:T(8,128)(2,1)} %band_ref.1) | copy-start | bytes 589828
  1.9 0.7 %copy-start.2 = (s32[8,8]{1,0:T(8,128)S(1)}, s32[8,8]{1,0:T(8,128)}, u32[]{:S(2)}) copy-start(s32[8,8]{1,0:T(8,128)} %pairs_ref.1) | copy-start | bytes 772

commit v3 on v2

--- a/solution.py
+++ b/solution.py
@@ -14,6 +14,7 @@
     rows, groups, coeff_ref, band_ref, pairs_ref, out_ref,
     coeffs, bands, halves, own_t, parts, arrived,
     cz_send, cs_send, ca_send, c_recv, bz_send, bs_send, b_recv, k_send, k_recv,
+    own_sem,
 ):
     chips = rows // 2
     occupied, block = coeff_ref.shape
@@ -43,11 +44,13 @@
             barrier, inc=1, device_id={"aux": lax.rem(group + shift, groups)}, device_id_type=MESH
         )
 
+    own_coeff = pltpu.make_async_copy(coeff_ref, coeffs.at[row + 1], own_sem.at[0])
+    own_band = pltpu.make_async_copy(band_ref, bands.at[row], own_sem.at[1])
+    own_coeff.start()
+    own_band.start()
     edge = jnp.zeros((occupied, block), coeffs.dtype)
     coeffs[0] = edge
     coeffs[rows + 1] = edge
-    coeffs[row + 1] = coeff_ref[...]
-    bands[row] = band_ref[...]
 
     sides = jnp.minimum(chip, 1) + jnp.minimum(chips - 1 - chip, 1)
     pl.semaphore_wait(barrier, groups + sides)
@@ -97,9 +100,11 @@
         for q in range(naux):
             band_on(row, q, side, target).start()
 
+    own_coeff.wait()
     each_side(start_coeff)
     for part in range(2):
         coeff_other(row, part).start()
+    own_band.wait()
     each_side(start_band)
     for q in range(naux):
         band_other(row, q).start()
@@ -173,7 +178,7 @@
         parts[origin] = total
         pl.when(origin != group)(lambda: part_out(origin).start())
 
-    for step in range(1, min(chips, 3)):
+    for step in range(1, min(chips, 4)):
         relay_row(step)
     for part in range(2):
         coeff_other(other, part).wait_recv()
@@ -185,7 +190,7 @@
     multiply(chip)
 
     def forward(step, carry):
-        pl.when(step + 2 < chips)(lambda: relay_row(step + 2))
+        pl.when(step + 3 < chips)(lambda: relay_row(step + 3))
         pl.when(step + 1 < chips)(lambda: relay_groups(step + 1))
 
         for side, origin, ahead in sources(step):
@@ -257,12 +262,13 @@
     naux, depth, _ = band.shape
     chips = rows // 2
     dma = pltpu.SemaphoreType.DMA
+    held = pl.BlockSpec(memory_space=pl.ANY)
     vmem = pl.BlockSpec(memory_space=pltpu.VMEM)
     flops = 2 * rows * naux * occupied * block * (depth + block)
     return pl.pallas_call(
         functools.partial(exchange_kernel, rows, groups),
         out_shape=jax.ShapeDtypeStruct((block, 2 * block), jnp.float32),
-        in_specs=[vmem, vmem, pl.BlockSpec(memory_space=pltpu.SMEM)],
+        in_specs=[held, held, pl.BlockSpec(memory_space=pltpu.SMEM)],
         out_specs=vmem,
         scratch_shapes=[
             pltpu.VMEM((rows + 2, occupied, block), jnp.bfloat16),
@@ -273,7 +279,7 @@
             pltpu.VMEM((groups, block, 2 * block), jnp.float32),
             dma((2, rows, 2)), dma((rows, 2)), dma((chips, 2, groups - 1)), dma((rows, 2)),
             dma((2, rows, naux)), dma((rows, naux)), dma((rows, naux)),
-            dma((groups,)), dma((groups,)),
+            dma((groups,)), dma((groups,)), dma((2,)),
         ],
         compiler_params=pltpu.CompilerParams(
             collective_id=0, has_side_effects=True, vmem_limit_bytes=48 * 2**20

time: 40.9 us -> 39.9 us (0.976)
  the two profiles are of different devices: /device:TPU:25 before, /device:TPU:7 now
where the time goes in v3:
time: 39.9 us; the launch traced here: 39.7 us
  Pallas kernels  36.5 us (91%)
  local copies, waits for them, and re-layouts  3.2 us (8%)
    pallas_call x1, Pallas kernels, on_device(): pl.pallas_call(functools.partial(exchange_kernel, rows, groups), out_shap...  36.5 us
    unnamed x7, local copies, waits for them, and re-layouts  3.2 us

profile of v3, /device:TPU:7, one launch (start us, length us, event | category | flops | bytes accessed | tf_op | source)
XLA Modules:
  0.0 39.7 jit_solution(9368773252143568863)
XLA Ops:
  0.0 0.0 copy-start
  0.0 0.9 %copy-done = bf16[800,128]{1,0:T(8,128)(2,1)S(1)} copy-done((bf16[800,128]{1,0:T(8,128)(2,1)S(1)}, bf16[800,128]{1,0:T(8,128)(2,1)}, u32[]{:S(2)}) %copy-start) | copy-done | bytes 204824
  0.9 0.0 copy-start.1
  0.9 0.9 %copy-done.1 = bf16[2,384,128]{2,1,0:T(8,128)(2,1)S(1)} copy-done((bf16[2,384,128]{2,1,0:T(8,128)(2,1)S(1)}, bf16[2,384,128]{2,1,0:T(8,128)(2,1)}, u32[]{:S(2)}) %copy-start.1) | copy-done | bytes 196632
  1.9 0.0 copy-start.2
  1.9 0.7 %copy-done.2 = s32[8,8]{1,0:T(8,128)S(1)} copy-done((s32[8,8]{1,0:T(8,128)S(1)}, s32[8,8]{1,0:T(8,128)}, u32[]{:S(2)}) %copy-start.2) | copy-done | bytes 280
  2.5 36.5 %shard_map.37 = f32[128,256]{1,0:T(8,128)S(1)} custom-call(bf16[800,128]{1,0:T(8,128)(2,1)S(1)} %copy-done, bf16[2,384,128]{2,1,0:T(8,128)(2,1)S(1)} %copy-done.1, s32[8,8]{1,0:T(8,128)S(1)} %copy-done.2), custom_call_target="tpu_custom_call" | custom-call | flops 1677721600 | bytes 1048576 | tf_op jit(solution)/shard_map/pallas_call | solution.py:268
  39.1 0.7 %copy.5 = f32[128,256]{1,0:T(8,128)} copy(f32[128,256]{1,0:T(8,128)S(1)} %shard_map.37) | data formatting | bytes 262144
Async XLA Ops:
  0.0 0.9 %copy-start = (bf16[800,128]{1,0:T(8,128)(2,1)S(1)}, bf16[800,128]{1,0:T(8,128)(2,1)}, u32[]{:S(2)}) copy-start(bf16[800,128]{1,0:T(8,128)(2,1)} %coeff_ref.1) | copy-start | bytes 614404
  0.9 0.9 %copy-start.1 = (bf16[2,384,128]{2,1,0:T(8,128)(2,1)S(1)}, bf16[2,384,128]{2,1,0:T(8,128)(2,1)}, u32[]{:S(2)}) copy-start(bf16[2,384,128]{2,1,0:T(8,128)(2,1)} %band_ref.1) | copy-start | bytes 589828
  1.9 0.7 %copy-start.2 = (s32[8,8]{1,0:T(8,128)S(1)}, s32[8,8]{1,0:T(8,128)}, u32[]{:S(2)}) copy-start(s32[8,8]{1,0:T(8,128)} %pairs_ref.1) | copy-start | bytes 772

commit v4 on v3

--- a/solution.py
+++ b/solution.py
@@ -178,14 +178,17 @@
         parts[origin] = total
         pl.when(origin != group)(lambda: part_out(origin).start())
 
-    for step in range(1, min(chips, 4)):
-        relay_row(step)
+    relay_row(1)
     for part in range(2):
         coeff_other(other, part).wait_recv()
-    relay_groups(1)
     for q in range(naux):
         band_other(other, q).wait_recv()
+    if chips > 2:
+        relay_row(2)
+    relay_groups(1)
     half_pair(chip)
+    if chips > 3:
+        relay_row(3)
     own_t[...] = halves[core].T
     multiply(chip)
 

time: 39.9 us -> 38.5 us (0.965)
  the two profiles are of different devices: /device:TPU:7 before, /device:TPU:25 now
where the time goes in v4:
time: 38.5 us; the launch traced here: 38.3 us
  Pallas kernels  35.1 us (91%)
  local copies, waits for them, and re-layouts  3.2 us (8%)
    pallas_call x1, Pallas kernels, on_device(): pl.pallas_call(functools.partial(exchange_kernel, rows, groups), out_shap...  35.1 us
    unnamed x7, local copies, waits for them, and re-layouts  3.2 us

profile of v4, /device:TPU:25, one launch (start us, length us, event | category | flops | bytes accessed | tf_op | source)
XLA Modules:
  0.0 38.3 jit_solution(3034899957416730376)
XLA Ops:
  0.0 0.0 copy-start
  0.0 0.9 %copy-done = bf16[800,128]{1,0:T(8,128)(2,1)S(1)} copy-done((bf16[800,128]{1,0:T(8,128)(2,1)S(1)}, bf16[800,128]{1,0:T(8,128)(2,1)}, u32[]{:S(2)}) %copy-start) | copy-done | bytes 204824
  0.9 0.0 copy-start.1
  0.9 0.9 %copy-done.1 = bf16[2,384,128]{2,1,0:T(8,128)(2,1)S(1)} copy-done((bf16[2,384,128]{2,1,0:T(8,128)(2,1)S(1)}, bf16[2,384,128]{2,1,0:T(8,128)(2,1)}, u32[]{:S(2)}) %copy-start.1) | copy-done | bytes 196632
  1.9 0.0 copy-start.2
  1.9 0.7 %copy-done.2 = s32[8,8]{1,0:T(8,128)S(1)} copy-done((s32[8,8]{1,0:T(8,128)S(1)}, s32[8,8]{1,0:T(8,128)}, u32[]{:S(2)}) %copy-start.2) | copy-done | bytes 280
  2.5 35.1 %shard_map.37 = f32[128,256]{1,0:T(8,128)S(1)} custom-call(bf16[800,128]{1,0:T(8,128)(2,1)S(1)} %copy-done, bf16[2,384,128]{2,1,0:T(8,128)(2,1)S(1)} %copy-done.1, s32[8,8]{1,0:T(8,128)S(1)} %copy-done.2), custom_call_target="tpu_custom_call" | custom-call | flops 1677721600 | bytes 1048576 | tf_op jit(solution)/shard_map/pallas_call | solution.py:271
  37.7 0.7 %copy.5 = f32[128,256]{1,0:T(8,128)} copy(f32[128,256]{1,0:T(8,128)S(1)} %shard_map.37) | data formatting | bytes 262144
Async XLA Ops:
  0.0 0.9 %copy-start = (bf16[800,128]{1,0:T(8,128)(2,1)S(1)}, bf16[800,128]{1,0:T(8,128)(2,1)}, u32[]{:S(2)}) copy-start(bf16[800,128]{1,0:T(8,128)(2,1)} %coeff_ref.1) | copy-start | bytes 614404
  0.9 0.9 %copy-start.1 = (bf16[2,384,128]{2,1,0:T(8,128)(2,1)S(1)}, bf16[2,384,128]{2,1,0:T(8,128)(2,1)}, u32[]{:S(2)}) copy-start(bf16[2,384,128]{2,1,0:T(8,128)(2,1)} %band_ref.1) | copy-start | bytes 589828
  1.9 0.7 %copy-start.2 = (s32[8,8]{1,0:T(8,128)S(1)}, s32[8,8]{1,0:T(8,128)}, u32[]{:S(2)}) copy-start(s32[8,8]{1,0:T(8,128)} %pairs_ref.1) | copy-start | bytes 772

commit v5 on v4

--- a/solution.py
+++ b/solution.py
@@ -14,7 +14,7 @@
     rows, groups, coeff_ref, band_ref, pairs_ref, out_ref,
     coeffs, bands, halves, own_t, parts, arrived,
     cz_send, cs_send, ca_send, c_recv, bz_send, bs_send, b_recv, k_send, k_recv,
-    own_sem,
+    own_sem, kept_pairs,
 ):
     chips = rows // 2
     occupied, block = coeff_ref.shape
@@ -48,6 +48,8 @@
     own_band = pltpu.make_async_copy(band_ref, bands.at[row], own_sem.at[1])
     own_coeff.start()
     own_band.start()
+    own_pairs = pltpu.make_async_copy(pairs_ref, kept_pairs, own_sem.at[2])
+    own_pairs.start()
     edge = jnp.zeros((occupied, block), coeffs.dtype)
     coeffs[0] = edge
     coeffs[rows + 1] = edge
@@ -108,6 +110,7 @@
     each_side(start_band)
     for q in range(naux):
         band_other(row, q).start()
+    own_pairs.wait()
 
     def sources(step):
         return ((0, chip - step, chip + 1), (1, chip + step, chip - 1))
@@ -215,7 +218,7 @@
              {"aux": giver}).wait_recv()
         total = total + arrived[giver]
     for j in range(2):
-        kept = pairs_ref[row, group * 2 + j].astype(jnp.float32)
+        kept = kept_pairs[row, group * 2 + j].astype(jnp.float32)
         out_ref[:, j * block:(j + 1) * block] = total[:, j * block:(j + 1) * block] * kept
 
     def left_own(side, target):
@@ -271,7 +274,7 @@
     return pl.pallas_call(
         functools.partial(exchange_kernel, rows, groups),
         out_shape=jax.ShapeDtypeStruct((block, 2 * block), jnp.float32),
-        in_specs=[held, held, pl.BlockSpec(memory_space=pltpu.SMEM)],
+        in_specs=[held, held, held],
         out_specs=vmem,
         scratch_shapes=[
             pltpu.VMEM((rows + 2, occupied, block), jnp.bfloat16),
@@ -282,7 +285,8 @@
             pltpu.VMEM((groups, block, 2 * block), jnp.float32),
             dma((2, rows, 2)), dma((rows, 2)), dma((chips, 2, groups - 1)), dma((rows, 2)),
             dma((2, rows, naux)), dma((rows, naux)), dma((rows, naux)),
-            dma((groups,)), dma((groups,)), dma((2,)),
+            dma((groups,)), dma((groups,)), dma((3,)),
+            pltpu.SMEM((rows, rows), jnp.int32),
         ],
         compiler_params=pltpu.CompilerParams(
             collective_id=0, has_side_effects=True, vmem_limit_bytes=48 * 2**20

time: 38.5 us -> 37.9 us (0.984)
  Pallas kernels: 35.1 us -> 34.5 us
    pallas_call x1, Pallas kernels: 35.1 us -> 34.5 us  [on_device(): pl.pallas_call(functools.partial(exchange_kernel, rows, groups), out_shap...]
where the time goes in v5:
time: 37.9 us; the launch traced here: 37.7 us
  Pallas kernels  34.5 us (91%)
  local copies, waits for them, and re-layouts  3.2 us (8%)
    pallas_call x1, Pallas kernels, on_device(): pl.pallas_call(functools.partial(exchange_kernel, rows, groups), out_shap...  34.5 us
    unnamed x7, local copies, waits for them, and re-layouts  3.2 us

profile of v5, /device:TPU:25, one launch (start us, length us, event | category | flops | bytes accessed | tf_op | source)
XLA Modules:
  0.0 37.7 jit_solution(2095410041700902259)
XLA Ops:
  0.0 0.0 copy-start
  0.0 0.9 %copy-done = bf16[800,128]{1,0:T(8,128)(2,1)S(1)} copy-done((bf16[800,128]{1,0:T(8,128)(2,1)S(1)}, bf16[800,128]{1,0:T(8,128)(2,1)}, u32[]{:S(2)}) %copy-start) | copy-done | bytes 204824
  0.9 0.0 copy-start.1
  0.9 0.9 %copy-done.1 = bf16[2,384,128]{2,1,0:T(8,128)(2,1)S(1)} copy-done((bf16[2,384,128]{2,1,0:T(8,128)(2,1)S(1)}, bf16[2,384,128]{2,1,0:T(8,128)(2,1)}, u32[]{:S(2)}) %copy-start.1) | copy-done | bytes 196632
  1.9 0.0 copy-start.2
  1.9 0.7 %copy-done.2 = s32[8,8]{1,0:T(8,128)S(1)} copy-done((s32[8,8]{1,0:T(8,128)S(1)}, s32[8,8]{1,0:T(8,128)}, u32[]{:S(2)}) %copy-start.2) | copy-done | bytes 280
  2.5 34.5 %shard_map.37 = f32[128,256]{1,0:T(8,128)S(1)} custom-call(bf16[800,128]{1,0:T(8,128)(2,1)S(1)} %copy-done, bf16[2,384,128]{2,1,0:T(8,128)(2,1)S(1)} %copy-done.1, s32[8,8]{1,0:T(8,128)S(1)} %copy-done.2), custom_call_target="tpu_custom_call" | custom-call | flops 1677721600 | bytes 1048576 | tf_op jit(solution)/shard_map/pallas_call | solution.py:274
  37.1 0.7 %copy.5 = f32[128,256]{1,0:T(8,128)} copy(f32[128,256]{1,0:T(8,128)S(1)} %shard_map.37) | data formatting | bytes 262144
Async XLA Ops:
  0.0 0.9 %copy-start = (bf16[800,128]{1,0:T(8,128)(2,1)S(1)}, bf16[800,128]{1,0:T(8,128)(2,1)}, u32[]{:S(2)}) copy-start(bf16[800,128]{1,0:T(8,128)(2,1)} %coeff_ref.1) | copy-start | bytes 614404
  0.9 0.9 %copy-start.1 = (bf16[2,384,128]{2,1,0:T(8,128)(2,1)S(1)}, bf16[2,384,128]{2,1,0:T(8,128)(2,1)}, u32[]{:S(2)}) copy-start(bf16[2,384,128]{2,1,0:T(8,128)(2,1)} %band_ref.1) | copy-start | bytes 589828
  1.9 0.7 %copy-start.2 = (s32[8,8]{1,0:T(8,128)S(1)}, s32[8,8]{1,0:T(8,128)}, u32[]{:S(2)}) copy-start(s32[8,8]{1,0:T(8,128)} %pairs_ref.1) | copy-start | bytes 772
